TPU v7x, 32 devices: a whole 2x2x4 slice. The times are simulated.
32 devices in a mesh: seq: 8 (over z, core), rep: 4 (over y, x).
Axes of the slice: x: 2, y: 2, z: 4, core: 2. Of those that a mesh axis runs over, the one named last changes fastest.
Arguments:
- probe_vectors: bfloat16 [4, 1024, 1024], P('rep', 'seq'), may hold values from -200 to 200
- lookup_vectors: bfloat16 [4, 1024, 1024], P('rep', 'seq'), may hold values from -9 to 9
- content_vectors: bfloat16 [4, 1024, 1024], P('rep', 'seq'), may hold values from -6 to 6
- recursion_levels: int32 [4, 1024], P('rep', 'seq'), may hold values from 1 to 3, as said below
- routing_preactivations: float32 [4, 1024], P('rep', 'seq'), may hold values from -6 to 6
- attender_multiplier: float32 [8], replicated, may hold values from 0.5 to 2
- upstream_adjoint: bfloat16 [4, 256, 1024], P('rep', 'seq'), may hold values from -20 to 20
Outputs:
- mixed_rows: bfloat16 [4, 256, 1024], P('rep', 'seq')
- gate_grad: float32 [4, 256], P('rep', 'seq')
- query_grad: bfloat16 [4, 256, 1024], P('rep', 'seq')
- key_grad: bfloat16 [4, 256, 1024], P('rep', 'seq')
- value_grad: bfloat16 [4, 256, 1024], P('rep', 'seq')
- attender_multiplier_derivative: float32 [8], P('seq')
Inputs may be any that keep to these rules, and one draw needn't show every extreme that they name: `recursion_levels`: in each block of 128 tokens at least one and at most 32 tokens have depths over 2; in every draw some block has exactly 32.
All inputs are finite; a program needn't handle non-finite values.
Results may differ from a plain program's by a relative error of at most 0.0058.
Values may be sent and summed in bfloat16 or wider, within the bound.
A program may use at most 64 MiB of HBM per device.

v0:
```python
import math

import jax
import jax.numpy as jnp
from jax import lax
from jax.sharding import PartitionSpec as P

STEP = 2


def compact_slots(depth_line, capacity):
    active = depth_line > STEP
    flags = active.astype(jnp.int32)
    ranked = jnp.cumsum(flags) - 1
    slot_ids = jnp.arange(capacity, dtype=jnp.int32)
    matched = (ranked[None, :] == slot_ids[:, None]) & active[None, :]
    places = jnp.arange(depth_line.shape[0], dtype=jnp.int32)
    slot_rows = jnp.sum(jnp.where(matched, places[None, :], 0), axis=1)
    live_count = jnp.sum(flags)
    return (slot_rows, slot_ids < live_count, live_count)


def pick_rows(table, slot_rows, is_live):
    picked = jnp.take(table, slot_rows, axis=0)
    return jnp.where(is_live[:, None], picked, jnp.zeros_like(picked))


def local(
    probe_vectors,
    lookup_vectors,
    content_vectors,
    recursion_levels,
    routing_preactivations,
    attender_multiplier,
    upstream_adjoint,
):
    capacity = upstream_adjoint.shape[1]
    width = probe_vectors.shape[2]
    attender_amount = attender_multiplier.shape[0]
    head_size = width // attender_amount
    group_size = lax.axis_size("seq")
    total_rows = group_size * capacity
    block_rows = min(total_rows, 512)
    block_count = total_rows // block_rows
    weighted_similarity = 1.0 / math.sqrt(head_size)
    slot_rows, is_live, live_count = compact_slots(recursion_levels[0], capacity)

    def head_layout():
        part_q = pick_rows(probe_vectors[0], slot_rows, is_live).reshape(
            capacity, attender_amount, head_size
        )
        part_k = pick_rows(lookup_vectors[0], slot_rows, is_live).reshape(
            capacity, attender_amount, head_size
        )
        part_v = pick_rows(content_vectors[0], slot_rows, is_live).reshape(
            capacity, attender_amount, head_size
        )
        return (part_q, part_k, part_v)

    first_q, first_k, first_v = head_layout()
    got_q, got_k, got_v = (
        lax.all_to_all(first_q, "seq", split_axis=1, concat_axis=0, tiled=True),
        lax.all_to_all(first_k, "seq", split_axis=1, concat_axis=0, tiled=True),
        lax.all_to_all(first_v, "seq", split_axis=1, concat_axis=0, tiled=True),
    )
    head_q = got_q.reshape(total_rows, head_size)
    head_k = got_k.reshape(total_rows, head_size)
    head_v = got_v.reshape(total_rows, head_size)
    counts_all = lax.all_gather(live_count.reshape(1), "seq", axis=0, tiled=True)
    live_keys = (jnp.arange(capacity, dtype=jnp.int32)[None, :] < counts_all[:, None]).reshape(
        total_rows
    )
    lone_attender = lax.axis_index("seq")
    head_temp = jnp.sum(
        jnp.where(
            jnp.arange(attender_amount, dtype=jnp.int32) == lone_attender, attender_multiplier, 0.0
        )
    )
    row_order = jnp.arange(total_rows, dtype=jnp.int32)
    row_blocks = row_order.reshape(block_count, block_rows)

    def softmax_rows(q_block, rows_block, key_matrix):
        bare_similarity = (
            jnp.einsum("id,jd->ij", q_block, key_matrix, preferred_element_type=jnp.float32)
            * weighted_similarity
        )
        lower_triangle = live_keys[None, :] & (row_order[None, :] <= rows_block[:, None])
        multiplied_similarities = jnp.where(lower_triangle, head_temp * bare_similarity, -jnp.inf)
        row_max = jnp.max(multiplied_similarities, axis=1, keepdims=True)
        shifted = jnp.exp(multiplied_similarities - row_max)
        return (bare_similarity, shifted / jnp.sum(shifted, axis=1, keepdims=True))

    def forward_block(iteration_arguments):
        q_block, rows_block = iteration_arguments
        bare_similarity, probs = softmax_rows(q_block, rows_block, head_k)
        return jnp.dot(
            probs.astype(jnp.bfloat16), head_v, preferred_element_type=jnp.float32
        ).astype(jnp.bfloat16)

    attended = lax.map(
        forward_block, (head_q.reshape(block_count, block_rows, head_size), row_blocks)
    )
    back_rows = lax.all_to_all(
        attended.reshape(total_rows, 1, head_size), "seq", split_axis=0, concat_axis=1, tiled=True
    )
    attn_wide = back_rows.reshape(capacity, width).astype(jnp.float32)
    picked_logits = jnp.take(routing_preactivations[0], slot_rows)
    sigmoid_gate = jax.nn.sigmoid(picked_logits)
    gate_value = jnp.where(is_live, sigmoid_gate, 0.0)
    mixed_rows = (gate_value[:, None] * attn_wide).astype(jnp.bfloat16)
    cot_wide = upstream_adjoint[0].astype(jnp.float32)
    gate_grad = jnp.where(
        is_live, sigmoid_gate * (1.0 - sigmoid_gate) * jnp.sum(cot_wide * attn_wide, axis=1), 0.0
    )
    upstream = (
        (gate_value[:, None] * cot_wide)
        .astype(jnp.bfloat16)
        .reshape(capacity, attender_amount, head_size)
    )
    head_grad = lax.all_to_all(upstream, "seq", split_axis=1, concat_axis=0, tiled=True).reshape(
        total_rows, head_size
    )
    again_q, again_k, again_v = head_layout()
    back_q, back_k, back_v = (
        lax.all_to_all(again_q, "seq", split_axis=1, concat_axis=0, tiled=True),
        lax.all_to_all(again_k, "seq", split_axis=1, concat_axis=0, tiled=True),
        lax.all_to_all(again_v, "seq", split_axis=1, concat_axis=0, tiled=True),
    )
    use_q = back_q.reshape(total_rows, head_size)
    use_k = back_k.reshape(total_rows, head_size)
    use_v = back_v.reshape(total_rows, head_size)

    def backward_block(running_state, iteration_arguments):
        lookup_summed, content_summed, multiplier_summed = running_state
        q_block, grad_block, rows_block = iteration_arguments
        bare_similarity, probs = softmax_rows(q_block, rows_block, use_k)
        grad_probs = jnp.einsum("id,jd->ij", grad_block, use_v, preferred_element_type=jnp.float32)
        inner_sum = jnp.sum(probs * grad_probs, axis=1, keepdims=True)
        similarity_derivative = probs * (grad_probs - inner_sum)
        multiplier_summed = multiplier_summed + jnp.sum(similarity_derivative * bare_similarity)
        bare_derivative = (similarity_derivative * (head_temp * weighted_similarity)).astype(
            jnp.bfloat16
        )
        probe_tile = jnp.dot(bare_derivative, use_k, preferred_element_type=jnp.float32).astype(
            jnp.bfloat16
        )
        lookup_summed = lookup_summed + jnp.einsum(
            "ij,id->jd", bare_derivative, q_block, preferred_element_type=jnp.float32
        )
        content_summed = content_summed + jnp.einsum(
            "ij,id->jd", probs.astype(jnp.bfloat16), grad_block, preferred_element_type=jnp.float32
        )
        return ((lookup_summed, content_summed, multiplier_summed), probe_tile)

    start_state = (
        jnp.zeros((total_rows, head_size), jnp.float32),
        jnp.zeros((total_rows, head_size), jnp.float32),
        jnp.zeros((), jnp.float32),
    )
    looped_result = lax.scan(
        backward_block,
        start_state,
        (
            use_q.reshape(block_count, block_rows, head_size),
            head_grad.reshape(block_count, block_rows, head_size),
            row_blocks,
        ),
    )
    (lookup_summed, content_summed, multiplier_summed), probe_tiles = looped_result
    attender_multiplier_derivative = lax.psum(multiplier_summed.reshape(1), "rep")
    grad_q_heads = probe_tiles.reshape(total_rows, 1, head_size)
    grad_k_heads = lookup_summed.astype(jnp.bfloat16).reshape(total_rows, 1, head_size)
    grad_v_heads = content_summed.astype(jnp.bfloat16).reshape(total_rows, 1, head_size)
    grads_q, grads_k, grads_v = (
        lax.all_to_all(grad_q_heads, "seq", split_axis=0, concat_axis=1, tiled=True),
        lax.all_to_all(grad_k_heads, "seq", split_axis=0, concat_axis=1, tiled=True),
        lax.all_to_all(grad_v_heads, "seq", split_axis=0, concat_axis=1, tiled=True),
    )
    return (
        mixed_rows[None],
        gate_grad[None],
        grads_q.reshape(1, capacity, width),
        grads_k.reshape(1, capacity, width),
        grads_v.reshape(1, capacity, width),
        attender_multiplier_derivative,
    )


def solution(mesh):
    in_specs = (
        P("rep", "seq", None),
        P("rep", "seq", None),
        P("rep", "seq", None),
        P("rep", "seq"),
        P("rep", "seq"),
        P(),
        P("rep", "seq", None),
    )
    out_specs = (
        P("rep", "seq", None),
        P("rep", "seq"),
        P("rep", "seq", None),
        P("rep", "seq", None),
        P("rep", "seq", None),
        P("seq"),
    )
    return jax.shard_map(local, mesh=mesh, in_specs=in_specs, out_specs=out_specs, check_vma=False)
```

profile of v0, /device:TPU:0, one launch (start us, length us, event | category | flops | bytes accessed | tf_op | source)
XLA Modules:
  0.0 104.8 jit_solution(13091522417910357208)
XLA Ops:
  0.7 0.7 copy-done.5
  1.3 0.7 fusion.21
  2.0 0.1 copy.77
  2.1 0.2 reduce-window.8
  2.3 0.1 add_reduce_fusion
  2.4 0.1 select_reduce_fusion
  2.6 0.6 iota_compare_fusion.3
  3.2 0.6 copy-done.1
  3.9 0.7 gather_fusion
  4.6 0.6 divide_select_fusion
  5.2 0.6 gather_fusion.3
  5.8 0.3 copy-done.2
  6.2 0.6 gather_fusion.2
  6.8 0.3 copy-done.3
  7.1 0.6 gather_fusion.1
  7.8 0.6 copy.104
  8.5 0.7 copy-done.7
  9.1 0.6 dynamic-slice
  9.7 1.4 %dynamic-update-slice = s32[8]{0:T(128)S(1)} dynamic-update-slice(s32[8]{0:T(128)S(1)} %broadcast.199, s32[1]{0:T(128)} %bitcast.5, u32[]{:T(128)} %bitcast.6) | dynamic-update-slice | bytes 12
  11.1 6.3 %all-to-all-start.1 = ((bf16[32,8,128]{2,0,1:T(8,128)(2,1)}), bf16[32,8,128]{2,0,1:T(8,128)(2,1)S(1)}, u32[]{:S(2)}, u32[]{:S(2)}) async-start(bf16[32,8,128]{2,0,1:T(8,128)(2,1)} %bitcast.122), calls=%async_computation.1 | async-start | bytes 131072 | tf_op jit(solution)/shard_map/all_to_all | solution.py:63
  17.4 9.4 %all-reduce = s32[8]{0:T(128)S(1)} all-reduce(s32[8]{0:T(128)S(1)} %dynamic-update-slice), channel_id=1, replica_groups=mesh['seq'=8,'rep'=4] {'seq'}, use_global_device_ids=true, to_apply=%add | all-reduce | flops 8 | bytes 64
  26.8 0.6 copy.105
  27.4 0.2 copy-done.4
  27.8 3.4 %all-to-all-start = ((bf16[32,8,128]{2,0,1:T(8,128)(2,1)}), bf16[32,8,128]{2,0,1:T(8,128)(2,1)S(1)}, u32[]{:S(2)}, u32[]{:S(2)}) async-start(bf16[32,8,128]{2,0,1:T(8,128)(2,1)} %bitcast.123), calls=%async_computation | async-start | bytes 131072 | tf_op jit(solution)/shard_map/all_to_all | solution.py:62
  31.3 0.6 copy.103
  32.0 0.6 copy.84
  32.6 0.6 fusion.18
  33.9 3.1 %all-to-all-done = bf16[32,8,128]{2,0,1:T(8,128)(2,1)S(1)} async-done(((bf16[32,8,128]{2,0,1:T(8,128)(2,1)}), bf16[32,8,128]{2,0,1:T(8,128)(2,1)S(1)}, u32[]{:S(2)}, u32[]{:S(2)}) %all-to-all-start) | async-done | bytes 65568 | tf_op jit(solution)/shard_map/all_to_all | solution.py:62
  37.0 3.4 %all-to-all-start.4 = ((bf16[32,8,128]{2,0,1:T(8,128)(2,1)}), bf16[32,8,128]{2,0,1:T(8,128)(2,1)S(1)}, u32[]{:S(2)}, u32[]{:S(2)}) async-start(bf16[32,8,128]{2,0,1:T(8,128)(2,1)} %copy.84), calls=%async_computation.4 | async-start | bytes 131072 | tf_op jit(solution)/shard_map/all_to_all | solution.py:120
  40.4 0.2 fusion.7
  40.6 0.1 fusion.6
  40.7 5.5 %all-to-all-done.4 = bf16[32,8,128]{2,0,1:T(8,128)(2,1)S(1)} async-done(((bf16[32,8,128]{2,0,1:T(8,128)(2,1)}), bf16[32,8,128]{2,0,1:T(8,128)(2,1)S(1)}, u32[]{:S(2)}, u32[]{:S(2)}) %all-to-all-start.4) | async-done | bytes 65568 | tf_op jit(solution)/shard_map/all_to_all | solution.py:120
  46.2 3.4 %all-to-all-start.2 = ((bf16[32,8,128]{2,0,1:T(8,128)(2,1)}), bf16[32,8,128]{2,0,1:T(8,128)(2,1)S(1)}, u32[]{:S(2)}, u32[]{:S(2)}) async-start(bf16[32,8,128]{2,0,1:T(8,128)(2,1)} %bitcast.121), calls=%async_computation.2 | async-start | bytes 131072 | tf_op jit(solution)/shard_map/all_to_all | solution.py:64
  49.6 0.3 fusion.3
  49.8 5.6 %all-to-all-done.2 = bf16[32,8,128]{2,0,1:T(8,128)(2,1)S(1)} async-done(((bf16[32,8,128]{2,0,1:T(8,128)(2,1)}), bf16[32,8,128]{2,0,1:T(8,128)(2,1)S(1)}, u32[]{:S(2)}, u32[]{:S(2)}) %all-to-all-start.2) | async-done | bytes 65568 | tf_op jit(solution)/shard_map/all_to_all | solution.py:64
  55.4 0.3 fusion
  55.8 0.2 multiply_reduce_fusion.1
  56.0 0.5 broadcast.220
  56.5 0.7 reduce.6
  57.2 0.6 reshape.360
  57.8 3.4 %all-to-all-start.7 = ((bf16[8,2,2048]{2,1,0:T(2,128)(2,1)}), bf16[8,2,2048]{2,1,0:T(2,128)(2,1)S(1)}, u32[]{:S(2)}, u32[]{:S(2)}) async-start(bf16[8,2,2048]{2,1,0:T(2,128)(2,1)} %reshape.360), calls=%async_computation.7 | async-start | bytes 131072 | tf_op jit(solution)/shard_map/all_to_all | solution.py:177
  61.2 0.7 reduce.3
  61.8 0.6 reshape.354
  62.5 0.8 multiply_reduce_fusion
  63.3 10.5 %psum.7 = f32[1]{0:T(128)} all-reduce(f32[1]{0:T(128)} %bitcast.44), channel_id=1, replica_groups=mesh['seq'=8,'rep'=4] {'rep'}, use_global_device_ids=true, to_apply=%region_9.11 | all-reduce | flops 1 | bytes 8 | tf_op jit(solution)/shard_map/psum | solution.py:170
  73.8 0.2 fusion.1
  74.0 0.7 reduce.4
  74.7 5.0 %all-to-all-start.3 = ((bf16[8,2,2048]{2,1,0:T(2,128)(2,1)}), bf16[8,2,2048]{2,1,0:T(2,128)(2,1)S(1)}, u32[]{:S(2)}, u32[]{:S(2)}) async-start(bf16[8,2,2048]{2,1,0:T(2,128)(2,1)} %reshape.354), calls=%async_computation.3 | async-start | bytes 131072 | tf_op jit(solution)/shard_map/all_to_all | solution.py:103
  79.7 0.2 fusion.2
  79.9 0.7 reduce.5
  80.6 0.6 reshape.358
  81.2 0.6 reshape.356
  82.0 0.7 reshape.298
  82.6 3.0 %all-to-all-done.3 = bf16[8,2,2048]{2,1,0:T(2,128)(2,1)S(1)} async-done(((bf16[8,2,2048]{2,1,0:T(2,128)(2,1)}), bf16[8,2,2048]{2,1,0:T(2,128)(2,1)S(1)}, u32[]{:S(2)}, u32[]{:S(2)}) %all-to-all-start.3) | async-done | bytes 65568 | tf_op jit(solution)/shard_map/all_to_all | solution.py:103
  85.7 3.3 %all-to-all-start.6 = ((bf16[8,2,2048]{2,1,0:T(2,128)(2,1)}), bf16[8,2,2048]{2,1,0:T(2,128)(2,1)S(1)}, u32[]{:S(2)}, u32[]{:S(2)}) async-start(bf16[8,2,2048]{2,1,0:T(2,128)(2,1)} %reshape.358), calls=%async_computation.6 | async-start | bytes 131072 | tf_op jit(solution)/shard_map/all_to_all | solution.py:176
  89.1 0.1 convert_element_type.109
  89.3 0.7 multiply_convert_fusion.1
  90.0 0.1 fusion.9
  90.2 4.7 %all-to-all-done.6 = bf16[8,2,2048]{2,1,0:T(2,128)(2,1)S(1)} async-done(((bf16[8,2,2048]{2,1,0:T(2,128)(2,1)}), bf16[8,2,2048]{2,1,0:T(2,128)(2,1)S(1)}, u32[]{:S(2)}, u32[]{:S(2)}) %all-to-all-start.6) | async-done | bytes 65568 | tf_op jit(solution)/shard_map/all_to_all | solution.py:176
  94.9 3.4 %all-to-all-start.5 = ((bf16[8,2,2048]{2,1,0:T(2,128)(2,1)}), bf16[8,2,2048]{2,1,0:T(2,128)(2,1)S(1)}, u32[]{:S(2)}, u32[]{:S(2)}) async-start(bf16[8,2,2048]{2,1,0:T(2,128)(2,1)} %reshape.356), calls=%async_computation.5 | async-start | bytes 131072 | tf_op jit(solution)/shard_map/all_to_all | solution.py:175
  98.3 0.7 reshape.296
  99.0 1.1 %compare_select_fusion.3 = f32[1,32]{1,0:T(1,128)} fusion(f32[32]{0:T(128)S(1)} %fusion.9, f32[32]{0:T(128)S(1)} %gather_fusion, s32[32]{0:T(128)S(1)} %select_reduce_fusion, s32[]{:T(128)} %fusion.21), kind=kLoop, calls=%fused_computation.52 | loop fusion | flops 480 | bytes 516 | tf_op jit(solution)/shard_map/jit(_where)/select_n | solution.py:112
  100.1 3.9 %all-to-all-done.5 = bf16[8,2,2048]{2,1,0:T(2,128)(2,1)S(1)} async-done(((bf16[8,2,2048]{2,1,0:T(2,128)(2,1)}), bf16[8,2,2048]{2,1,0:T(2,128)(2,1)S(1)}, u32[]{:S(2)}, u32[]{:S(2)}) %all-to-all-start.5) | async-done | bytes 65568 | tf_op jit(solution)/shard_map/all_to_all | solution.py:175
  104.2 0.7 reshape.294
  (36 shorter events, 1.0 us)
Async XLA Ops:
  0.6 4.6 %copy-start = (bf16[1,128,1024]{2,1,0:T(8,128)(2,1)S(1)}, bf16[1,128,1024]{2,1,0:T(8,128)(2,1)}, u32[]{:S(2)}) copy-start(bf16[1,128,1024]{2,1,0:T(8,128)(2,1)} %param.11) | copy-start | bytes 786436
  0.7 0.7 copy-start.5
  3.2 0.7 copy-start.1
  5.2 1.0 copy-start.2
  6.1 0.9 copy-start.3
  8.5 0.7 copy-start.7
  11.1 16.7 %all-to-all-start.1 = ((bf16[32,8,128]{2,0,1:T(8,128)(2,1)}), bf16[32,8,128]{2,0,1:T(8,128)(2,1)S(1)}, u32[]{:S(2)}, u32[]{:S(2)}) async-start(bf16[32,8,128]{2,0,1:T(8,128)(2,1)} %bitcast.122), calls=%async_computation.1 | async-start | bytes 131072 | tf_op jit(solution)/shard_map/all_to_all | solution.py:63
  26.8 0.8 copy-start.4
  27.8 9.2 %all-to-all-start = ((bf16[32,8,128]{2,0,1:T(8,128)(2,1)}), bf16[32,8,128]{2,0,1:T(8,128)(2,1)S(1)}, u32[]{:S(2)}, u32[]{:S(2)}) async-start(bf16[32,8,128]{2,0,1:T(8,128)(2,1)} %bitcast.123), calls=%async_computation | async-start | bytes 131072 | tf_op jit(solution)/shard_map/all_to_all | solution.py:62
  32.0 0.7 copy-start.6
  37.0 9.2 %all-to-all-start.4 = ((bf16[32,8,128]{2,0,1:T(8,128)(2,1)}), bf16[32,8,128]{2,0,1:T(8,128)(2,1)S(1)}, u32[]{:S(2)}, u32[]{:S(2)}) async-start(bf16[32,8,128]{2,0,1:T(8,128)(2,1)} %copy.84), calls=%async_computation.4 | async-start | bytes 131072 | tf_op jit(solution)/shard_map/all_to_all | solution.py:120
  46.2 9.2 %all-to-all-start.2 = ((bf16[32,8,128]{2,0,1:T(8,128)(2,1)}), bf16[32,8,128]{2,0,1:T(8,128)(2,1)S(1)}, u32[]{:S(2)}, u32[]{:S(2)}) async-start(bf16[32,8,128]{2,0,1:T(8,128)(2,1)} %bitcast.121), calls=%async_computation.2 | async-start | bytes 131072 | tf_op jit(solution)/shard_map/all_to_all | solution.py:64
  57.8 16.9 %all-to-all-start.7 = ((bf16[8,2,2048]{2,1,0:T(2,128)(2,1)}), bf16[8,2,2048]{2,1,0:T(2,128)(2,1)S(1)}, u32[]{:S(2)}, u32[]{:S(2)}) async-start(bf16[8,2,2048]{2,1,0:T(2,128)(2,1)} %reshape.360), calls=%async_computation.7 | async-start | bytes 131072 | tf_op jit(solution)/shard_map/all_to_all | solution.py:177
  74.7 11.0 %all-to-all-start.3 = ((bf16[8,2,2048]{2,1,0:T(2,128)(2,1)}), bf16[8,2,2048]{2,1,0:T(2,128)(2,1)S(1)}, u32[]{:S(2)}, u32[]{:S(2)}) async-start(bf16[8,2,2048]{2,1,0:T(2,128)(2,1)} %reshape.354), calls=%async_computation.3 | async-start | bytes 131072 | tf_op jit(solution)/shard_map/all_to_all | solution.py:103
  85.7 9.2 %all-to-all-start.6 = ((bf16[8,2,2048]{2,1,0:T(2,128)(2,1)}), bf16[8,2,2048]{2,1,0:T(2,128)(2,1)S(1)}, u32[]{:S(2)}, u32[]{:S(2)}) async-start(bf16[8,2,2048]{2,1,0:T(2,128)(2,1)} %reshape.358), calls=%async_computation.6 | async-start | bytes 131072 | tf_op jit(solution)/shard_map/all_to_all | solution.py:176
  94.9 9.2 %all-to-all-start.5 = ((bf16[8,2,2048]{2,1,0:T(2,128)(2,1)}), bf16[8,2,2048]{2,1,0:T(2,128)(2,1)S(1)}, u32[]{:S(2)}, u32[]{:S(2)}) async-start(bf16[8,2,2048]{2,1,0:T(2,128)(2,1)} %reshape.356), calls=%async_computation.5 | async-start | bytes 131072 | tf_op jit(solution)/shard_map/all_to_all | solution.py:175
where the time goes:
time: 106 us; the launch traced here: 105 us
  starting transfers between devices  31.5 us (30%)
  waiting for transfers between devices  25.8 us (24%)
  blocking collectives  19.9 us (19%)
  local copies, waits for them, and re-layouts  15.7 us (15%)
  other arithmetic  8.87 us (8%)
  between operations  1.63 us (2%)
  matrix products  1.42 us (1%)
    psum x1, blocking collectives, local(): lax.psum(multiplier_summed.reshape(1), 'rep')  10.5 us
    unnamed x1, blocking collectives  9.39 us
    unnamed x31, local copies, waits for them, and re-layouts  7.7 us
    all_to_all x1, starting transfers between devices, local(): lax.all_to_all(first_k, 'seq', split_axis=1, concat_axis=0, tiled=True)  6.33 us
    all_to_all x1, waiting for transfers between devices, local(): lax.all_to_all(first_v, 'seq', split_axis=1, concat_axis=0, tiled=True)  5.58 us
    all_to_all x1, waiting for transfers between devices, local(): lax.all_to_all(upstream, 'seq', split_axis=1, concat_axis=0, tiled=True)  5.48 us
    all_to_all x1, starting transfers between devices, local(): lax.all_to_all(attended.reshape(total_rows, 1, head_size), 'seq', split_a...  5.04 us
    all_to_all x1, waiting for transfers between devices, local(): lax.all_to_all(grad_k_heads, 'seq', split_axis=0, concat_axis=1, tiled=True)  4.68 us
  transfers between devices with their start and end apart: 8, of which 6 were waited for; matrix products, arithmetic and copies ran while one was open for 12% of the time, Pallas kernels for 0%

commit v1 on v0

v1 whole, which is shorter than its diff:
```python
import functools
import math

import jax
import jax.numpy as jnp
from jax import lax
from jax.experimental import pallas as pl
from jax.experimental.pallas import tpu as pltpu
from jax.sharding import PartitionSpec as P

STEP = 2
MESH = pl.DeviceIdType.MESH
BF16 = jnp.bfloat16
F32 = jnp.float32


def kernel(
    n,
    reps,
    cap,
    hd,
    q_hbm,
    k_hbm,
    v_hbm,
    lev_hbm,
    logit_hbm,
    mult_ref,
    cot_hbm,
    mixed_ref,
    gg_ref,
    dq_ref,
    dk_ref,
    dv_ref,
    dm_ref,
    q_in,
    k_in,
    v_in,
    cot_in,
    lev_in,
    logit_in,
    send_a,
    send_b,
    send_c,
    recv_a,
    recv_b,
    recv_c,
    out_o,
    out_q,
    out_k,
    out_v,
    attn_in,
    dm_all,
    local_sem,
    send_sem,
    recv_sem,
    dm_send,
    dm_recv,
):
    me = lax.axis_index("seq")
    my_rep = lax.axis_index("rep")
    total = n * cap
    scale = 1.0 / math.sqrt(hd)

    def local_copy(src, dst, s):
        return pltpu.make_async_copy(src, dst, local_sem.at[s])

    lev_copy = local_copy(lev_hbm, lev_in, 0)
    logit_copy = local_copy(logit_hbm, logit_in, 1)
    q_copy = local_copy(q_hbm.at[0], q_in, 2)
    k_copy = local_copy(k_hbm.at[0], k_in, 3)
    v_copy = local_copy(v_hbm.at[0], v_in, 4)
    cot_copy = local_copy(cot_hbm.at[0], cot_in, 5)
    for c in (lev_copy, logit_copy, q_copy, k_copy, v_copy, cot_copy):
        c.start()

    def peer_loop(f):
        if n <= 8:
            for step in range(1, n):
                f(lax.rem(me + step, n))
        else:

            def body(step, carry):
                f(lax.rem(me + step, n))
                return carry

            lax.fori_loop(1, n, body, 0)

    barrier = pltpu.get_barrier_semaphore()
    peer_loop(
        lambda d: pl.semaphore_signal(
            barrier, inc=1, device_id={"seq": d}, device_id_type=MESH
        )
    )
    for r in range(1, reps):
        pl.semaphore_signal(
            barrier,
            inc=1,
            device_id={"rep": lax.rem(my_rep + r, reps)},
            device_id_type=MESH,
        )

    lev_copy.wait()
    tokens = lev_in.shape[1]
    active = lev_in[...] > STEP
    flags = jnp.where(active, 1.0, 0.0)
    upto = jnp.where(
        lax.broadcasted_iota(jnp.int32, (tokens, tokens), 0)
        <= lax.broadcasted_iota(jnp.int32, (tokens, tokens), 1),
        1.0,
        0.0,
    ).astype(BF16)
    ranked = jnp.dot(
        jnp.broadcast_to(flags, (16, tokens)).astype(BF16), upto, preferred_element_type=F32
    )[0:1] - 1.0
    slot_ids = lax.broadcasted_iota(jnp.int32, (cap, tokens), 0).astype(F32)
    matched = (ranked == slot_ids) & active
    chosen = jnp.where(matched, 1.0, 0.0)
    pick = chosen.astype(BF16)
    live = jnp.sum(chosen, axis=1, keepdims=True) > 0.5
    count = jnp.sum(flags, axis=1, keepdims=True)

    for h in range(n):
        send_a[h, 2 * cap :, :] = jnp.broadcast_to(count, (16, hd)).astype(BF16)

    def gather(src, dst, row):
        for c in range(0, n, 2):
            part = jnp.dot(
                pick, src[:, c * hd : (c + 2) * hd], preferred_element_type=F32
            ).astype(BF16)
            dst[c, row : row + cap, :] = part[:, :hd]
            dst[c + 1, row : row + cap, :] = part[:, hd:]

    def to_head(part, src, dst):
        def copy(d, slot):
            return pltpu.make_async_remote_copy(
                src_ref=src.at[d],
                dst_ref=dst.at[slot],
                send_sem=send_sem.at[part, d],
                recv_sem=recv_sem.at[part, slot],
                device_id={"seq": d},
                device_id_type=MESH,
            )

        return copy

    copy_a = to_head(0, send_a, recv_a)
    copy_b = to_head(1, send_b, recv_b)
    copy_c = to_head(2, send_c, recv_c)

    q_copy.wait()
    gather(q_in, send_a, 0)
    k_copy.wait()
    gather(k_in, send_a, cap)
    pl.semaphore_wait(barrier, n - 1 + reps - 1)
    peer_loop(lambda d: copy_a(d, me).start())
    recv_a[me] = send_a[me]

    v_copy.wait()
    gather(v_in, send_b, 0)
    peer_loop(lambda d: copy_b(d, me).start())
    recv_b[me] = send_b[me]

    logit_copy.wait()
    logits = jnp.sum(jnp.where(matched, logit_in[...], 0.0), axis=1, keepdims=True)
    sig = jax.nn.sigmoid(logits)
    gate = jnp.where(live, sig, 0.0)
    cot_copy.wait()
    for h in range(n):
        send_c[h] = (gate * cot_in[:, h * hd : (h + 1) * hd].astype(F32)).astype(BF16)
    peer_loop(lambda d: copy_c(d, me).start())
    recv_c[me] = send_c[me]

    temp = mult_ref[me]
    peer_loop(lambda d: copy_a(d, d).wait_recv())
    q_all = recv_a[:, 0:cap, :].reshape(total, hd)
    k_all = recv_a[:, cap : 2 * cap, :].reshape(total, hd)
    rows = min(total, 256)
    blocks = total // rows
    lane = lax.broadcasted_iota(jnp.int32, (1, hd), 1)
    per = hd // cap
    pieces = []
    for c in range(total // hd):
        counts = jnp.zeros((1, hd), F32)
        for b in range(per):
            got = recv_a[c * per + b, 2 * cap :, :].astype(F32)[0:1]
            counts = jnp.where(lane // cap == b, got, counts)
        pieces.append(jnp.where((lane % cap).astype(F32) < counts, 1.0, 0.0))
    live_keys = jnp.concatenate(pieces, axis=1) > 0.5

    NT = (((1,), (1,)), ((), ()))
    TN = (((0,), (0,)), ((), ()))
    plains, probs, lows = [], [], []
    for rb in range(blocks):
        end = (rb + 1) * rows
        plain = (
            lax.dot_general(
                q_all[rb * rows : end], k_all[:end], NT, preferred_element_type=F32
            )
            * scale
        )
        row_id = lax.broadcasted_iota(jnp.int32, (rows, end), 0) + rb * rows
        col_id = lax.broadcasted_iota(jnp.int32, (rows, end), 1)
        allowed = (col_id <= row_id) & live_keys[:, :end]
        scores = jnp.where(allowed, temp * plain, -jnp.inf)
        top = jnp.max(scores, axis=1, keepdims=True)
        shifted = jnp.exp(scores - top)
        prob = shifted * (1.0 / jnp.sum(shifted, axis=1, keepdims=True))
        plains.append(plain)
        probs.append(prob)
        lows.append(prob.astype(BF16))

    def to_slots(part, src, dst):
        def copy(d, slot):
            return pltpu.make_async_remote_copy(
                src_ref=src.at[pl.ds(pl.multiple_of(d * cap, cap), cap), :],
                dst_ref=dst.at[:, pl.ds(pl.multiple_of(slot * hd, hd), hd)],
                send_sem=send_sem.at[part, d],
                recv_sem=recv_sem.at[part, slot],
                device_id={"seq": d},
                device_id_type=MESH,
            )

        return copy

    copy_o = to_slots(3, out_o, attn_in)
    copy_v = to_slots(4, out_v, dv_ref.at[0])
    copy_q = to_slots(5, out_q, dq_ref.at[0])
    copy_k = to_slots(6, out_k, dk_ref.at[0])

    def finish(copy, src, dst):
        peer_loop(lambda d: copy(d, me).start())
        mine = src[pl.ds(pl.multiple_of(me * cap, cap), cap), :]
        dst[:, pl.ds(pl.multiple_of(me * hd, hd), hd)] = mine

    peer_loop(lambda d: copy_b(d, d).wait_recv())
    v_all = recv_b[...].reshape(total, hd)
    for rb in range(blocks):
        end = (rb + 1) * rows
        out_o[rb * rows : end, :] = jnp.dot(
            lows[rb], v_all[:end], preferred_element_type=F32
        ).astype(BF16)
    finish(copy_o, out_o, attn_in)

    peer_loop(lambda d: copy_c(d, d).wait_recv())
    u_all = recv_c[...].reshape(total, hd)

    def column_sums(left, right):
        tiles = [None] * blocks
        for rb in range(blocks):
            end = (rb + 1) * rows
            got = lax.dot_general(
                left[rb], right[rb * rows : end], TN, preferred_element_type=F32
            )
            for kb in range(rb + 1):
                tile = got[kb * rows : (kb + 1) * rows]
                tiles[kb] = tile if tiles[kb] is None else tiles[kb] + tile
        return tiles

    for kb, tile in enumerate(column_sums(lows, u_all)):
        out_v[kb * rows : (kb + 1) * rows, :] = tile.astype(BF16)
    finish(copy_v, out_v, dv_ref.at[0])

    lowered = []
    dm = jnp.zeros((1, 1), F32)
    for rb in range(blocks):
        end = (rb + 1) * rows
        grad_probs = lax.dot_general(
            u_all[rb * rows : end], v_all[:end], NT, preferred_element_type=F32
        )
        inner = jnp.sum(probs[rb] * grad_probs, axis=1, keepdims=True)
        grad_score = probs[rb] * (grad_probs - inner)
        by_row = jnp.sum(grad_score * plains[rb], axis=1, keepdims=True)
        dm = dm + jnp.sum(by_row, axis=0, keepdims=True)
        low = (grad_score * (temp * scale)).astype(BF16)
        lowered.append(low)
        out_q[rb * rows : end, :] = jnp.dot(
            low, k_all[:end], preferred_element_type=F32
        ).astype(BF16)
    finish(copy_q, out_q, dq_ref.at[0])
    for kb, tile in enumerate(column_sums(lowered, q_all)):
        out_k[kb * rows : (kb + 1) * rows, :] = tile.astype(BF16)
    finish(copy_k, out_k, dk_ref.at[0])

    dm_all[my_rep] = jnp.broadcast_to(dm, (8, 128))

    def copy_dm(r, slot):
        return pltpu.make_async_remote_copy(
            src_ref=dm_all.at[slot],
            dst_ref=dm_all.at[slot],
            send_sem=dm_send.at[r],
            recv_sem=dm_recv.at[slot],
            device_id={"rep": r},
            device_id_type=MESH,
        )

    for r in range(1, reps):
        copy_dm(lax.rem(my_rep + r, reps), my_rep).start()

    peer_loop(lambda d: copy_o(d, d).wait_recv())
    attn = attn_in[...].astype(F32)
    mixed_ref[0] = (gate * attn).astype(BF16)
    dots = jnp.sum(cot_in[...].astype(F32) * attn, axis=1, keepdims=True)
    grad_gate = jnp.where(live, sig * (1.0 - sig) * dots, 0.0)
    diagonal = lax.broadcasted_iota(jnp.int32, (cap, cap), 0) == lax.broadcasted_iota(
        jnp.int32, (cap, cap), 1
    )
    gg_ref[...] = jnp.sum(jnp.where(diagonal, grad_gate, 0.0), axis=0, keepdims=True)

    for r in range(1, reps):
        other = lax.rem(my_rep + r, reps)
        copy_dm(other, other).wait_recv()
    summed = dm_all[0]
    for r in range(1, reps):
        summed = summed + dm_all[r]
    dm_ref[...] = summed[0:1]

    for copy in (copy_v, copy_q, copy_k):
        peer_loop(lambda d: copy(d, d).wait_recv())
    for copy in (copy_a, copy_b, copy_c, copy_o, copy_v, copy_q, copy_k):
        peer_loop(lambda d: copy(d, me).wait_send())
    for r in range(1, reps):
        copy_dm(lax.rem(my_rep + r, reps), my_rep).wait_send()


def local(n, reps, q, k, v, levels, logits, mult, cot):
    tokens, width = q.shape[1], q.shape[2]
    cap = cot.shape[1]
    hd = width // mult.shape[0]
    total = n * cap
    anyspec = pl.BlockSpec(memory_space=pl.ANY)
    vm = pl.BlockSpec(memory_space=pltpu.VMEM)
    wide = jax.ShapeDtypeStruct((1, cap, width), BF16)
    outs = pl.pallas_call(
        functools.partial(kernel, n, reps, cap, hd),
        out_shape=(
            wide,
            jax.ShapeDtypeStruct((1, cap), F32),
            wide,
            wide,
            wide,
            jax.ShapeDtypeStruct((1, 128), F32),
        ),
        in_specs=[anyspec] * 5 + [pl.BlockSpec(memory_space=pltpu.SMEM), anyspec],
        out_specs=(vm,) * 6,
        scratch_shapes=[
            pltpu.VMEM((tokens, width), BF16),
            pltpu.VMEM((tokens, width), BF16),
            pltpu.VMEM((tokens, width), BF16),
            pltpu.VMEM((cap, width), BF16),
            pltpu.VMEM((1, tokens), jnp.int32),
            pltpu.VMEM((1, tokens), F32),
            pltpu.VMEM((n, 2 * cap + 16, hd), BF16),
            pltpu.VMEM((n, cap, hd), BF16),
            pltpu.VMEM((n, cap, hd), BF16),
            pltpu.VMEM((n, 2 * cap + 16, hd), BF16),
            pltpu.VMEM((n, cap, hd), BF16),
            pltpu.VMEM((n, cap, hd), BF16),
            pltpu.VMEM((total, hd), BF16),
            pltpu.VMEM((total, hd), BF16),
            pltpu.VMEM((total, hd), BF16),
            pltpu.VMEM((total, hd), BF16),
            pltpu.VMEM((cap, width), BF16),
            pltpu.VMEM((reps, 8, 128), F32),
            pltpu.SemaphoreType.DMA((6,)),
            pltpu.SemaphoreType.DMA((7, n)),
            pltpu.SemaphoreType.DMA((7, n)),
            pltpu.SemaphoreType.DMA((reps,)),
            pltpu.SemaphoreType.DMA((reps,)),
        ],
        compiler_params=pltpu.CompilerParams(
            collective_id=0, has_side_effects=True, vmem_limit_bytes=48 * 1024 * 1024
        ),
    )(q, k, v, levels, logits, mult, cot)
    mixed, gg, dq, dk, dv, dm = outs
    return mixed, gg, dq, dk, dv, dm[0, :1]


def solution(mesh):
    n, reps = mesh.shape["seq"], mesh.shape["rep"]
    in_specs = (
        P("rep", "seq", None),
        P("rep", "seq", None),
        P("rep", "seq", None),
        P("rep", "seq"),
        P("rep", "seq"),
        P(),
        P("rep", "seq", None),
    )
    out_specs = (
        P("rep", "seq", None),
        P("rep", "seq"),
        P("rep", "seq", None),
        P("rep", "seq", None),
        P("rep", "seq", None),
        P("seq"),
    )
    return jax.shard_map(
        functools.partial(local, n, reps),
        mesh=mesh,
        in_specs=in_specs,
        out_specs=out_specs,
        check_vma=False,
    )
```

time: 106 us -> 32.5 us (0.31)
  starting transfers between devices: 31.5 us -> 0 us
  waiting for transfers between devices: 25.8 us -> 0 us
  Pallas kernels: 0 us -> 21.7 us
  blocking collectives: 19.9 us -> 0 us
  other arithmetic: 8.87 us -> 0 us
  local copies, waits for them, and re-layouts: 15.7 us -> 8.67 us
  matrix products: 1.42 us -> 0 us
    all_to_all x8 -> x0, starting transfers between devices: 31.5 us -> none  [the longest x1 6.33 us: local(): lax.all_to_all(first_k, 'seq', split_axis=1, concat_axis=0, tiled=True)]
    all_to_all x8 -> x0, waiting for transfers between devices: 25.8 us -> none  [the longest x1 5.58 us: local(): lax.all_to_all(first_v, 'seq', split_axis=1, concat_axis=0, tiled=True)]
    pallas_call x0 -> x1, Pallas kernels: none -> 21.7 us  [local(): pl.pallas_call(functools.partial(kernel, n, reps, cap, hd), out_shape=(wi...]
    psum x1 -> x0, blocking collectives: 10.5 us -> none  [local(): lax.psum(multiplier_summed.reshape(1), 'rep')]
    unnamed x1 -> x0, blocking collectives: 9.39 us -> none
    reshape x7 -> x0, local copies, waits for them, and re-layouts: 4.43 us -> none  [the longest x1 0.66 us: local(): grads_v.reshape(1, capacity, width)]
    reshape x4 -> x0, other arithmetic: 2.65 us -> none  [the longest x1 0.66 us: local(): attended.reshape(total_rows, 1, head_size)]
    gather x4 -> x0, local copies, waits for them, and re-layouts: 2.58 us -> none  [the longest x3 1.88 us: pick_rows(): picked = jnp.take(table, slot_rows, axis=0)]
  transfers between devices with their start and end apart: 8 -> 0, of which waited for: 6 -> 0; matrix products, arithmetic and copies ran while one was open for 12% -> 0% of each run, Pallas kernels for 0% -> 0%
where the time goes in v1:
time: 32.5 us; the launch traced here: 32.2 us
  Pallas kernels  21.7 us (67%)
  local copies, waits for them, and re-layouts  8.67 us (27%)
  between operations  1.82 us (6%)
    pallas_call x1, Pallas kernels, local(): pl.pallas_call(functools.partial(kernel, n, reps, cap, hd), out_shape=(wi...  21.7 us
    unnamed x19, local copies, waits for them, and re-layouts  8.67 us

profile of v1, /device:TPU:0, one launch (start us, length us, event | category | flops | bytes accessed | tf_op | source)
XLA Modules:
  0.0 32.2 jit_solution(18312265240056304786)
XLA Ops:
  0.6 0.0 copy-start
  0.6 0.9 %copy-done = bf16[1,128,1024]{2,1,0:T(8,128)(2,1)S(1)} copy-done((bf16[1,128,1024]{2,1,0:T(8,128)(2,1)S(1)}, bf16[1,128,1024]{2,1,0:T(8,128)(2,1)}, u32[]{:S(2)}) %copy-start) | copy-done | bytes 262168
  1.6 0.0 copy-start.1
  1.6 0.9 %copy-done.1 = bf16[1,128,1024]{2,1,0:T(8,128)(2,1)S(1)} copy-done((bf16[1,128,1024]{2,1,0:T(8,128)(2,1)S(1)}, bf16[1,128,1024]{2,1,0:T(8,128)(2,1)}, u32[]{:S(2)}) %copy-start.1) | copy-done | bytes 262168
  2.5 0.0 copy-start.2
  2.5 0.9 %copy-done.2 = bf16[1,128,1024]{2,1,0:T(8,128)(2,1)S(1)} copy-done((bf16[1,128,1024]{2,1,0:T(8,128)(2,1)S(1)}, bf16[1,128,1024]{2,1,0:T(8,128)(2,1)}, u32[]{:S(2)}) %copy-start.2) | copy-done | bytes 262168
  3.5 0.0 copy-start.3
  3.5 0.8 %copy-done.3 = bf16[1,32,1024]{2,1,0:T(8,128)(2,1)S(1)} copy-done((bf16[1,32,1024]{2,1,0:T(8,128)(2,1)S(1)}, bf16[1,32,1024]{2,1,0:T(8,128)(2,1)}, u32[]{:S(2)}) %copy-start.3) | copy-done | bytes 65560
  4.3 0.0 copy-start.4
  4.3 0.7 %copy-done.4 = s32[1,128]{1,0:T(1,128)S(1)} copy-done((s32[1,128]{1,0:T(1,128)S(1)}, s32[1,128]{1,0:T(1,128)}, u32[]{:S(2)}) %copy-start.4) | copy-done | bytes 536
  5.0 0.0 copy-start.5
  5.0 0.7 %copy-done.5 = f32[1,128]{1,0:T(1,128)S(1)} copy-done((f32[1,128]{1,0:T(1,128)S(1)}, f32[1,128]{1,0:T(1,128)}, u32[]{:S(2)}) %copy-start.5) | copy-done | bytes 536
  5.6 0.0 copy-start.6
  5.6 0.7 %copy-done.6 = f32[8]{0:T(128)S(1)} copy-done((f32[8]{0:T(128)S(1)}, f32[8]{0:T(128)}, u32[]{:S(2)}) %copy-start.6) | copy-done | bytes 56
  6.3 21.7 %shard_map.118 = (bf16[1,32,1024]{2,1,0:T(8,128)(2,1)S(1)}, f32[1,32]{1,0:T(1,128)S(1)}, bf16[1,32,1024]{2,1,0:T(8,128)(2,1)S(1)}, bf16[1,32,1024]{2,1,0:T(8,128...) custom-call(bf16[1,128,1024]{2,1,0:T(8,128)(2,1)S(1)} %copy-done, ...), custom_call_target="tpu_custom_call" | custom-call | tf_op jit(solution)/shard_map/pallas_call | solution.py:333
  28.0 0.6 %copy.19 = bf16[1,32,1024]{2,1,0:T(8,128)(2,1)} copy(bf16[1,32,1024]{2,1,0:T(8,128)(2,1)S(1)} %get-tuple-element.24) | data formatting | bytes 131072
  28.7 0.5 %copy.20 = f32[1,32]{1,0:T(1,128)} copy(f32[1,32]{1,0:T(1,128)S(1)} %get-tuple-element.25) | data formatting | bytes 256
  29.2 0.6 %copy.21 = bf16[1,32,1024]{2,1,0:T(8,128)(2,1)} copy(bf16[1,32,1024]{2,1,0:T(8,128)(2,1)S(1)} %get-tuple-element.26) | data formatting | bytes 131072
  29.8 0.6 %copy.22 = bf16[1,32,1024]{2,1,0:T(8,128)(2,1)} copy(bf16[1,32,1024]{2,1,0:T(8,128)(2,1)S(1)} %get-tuple-element.27) | data formatting | bytes 131072
  30.4 0.6 %copy.23 = bf16[1,32,1024]{2,1,0:T(8,128)(2,1)} copy(bf16[1,32,1024]{2,1,0:T(8,128)(2,1)S(1)} %get-tuple-element.28) | data formatting | bytes 131072
Async XLA Ops:
  0.6 1.0 %copy-start = (bf16[1,128,1024]{2,1,0:T(8,128)(2,1)S(1)}, bf16[1,128,1024]{2,1,0:T(8,128)(2,1)}, u32[]{:S(2)}) copy-start(bf16[1,128,1024]{2,1,0:T(8,128)(2,1)} %q_hbm.1) | copy-start | bytes 786436
  1.6 0.9 %copy-start.1 = (bf16[1,128,1024]{2,1,0:T(8,128)(2,1)S(1)}, bf16[1,128,1024]{2,1,0:T(8,128)(2,1)}, u32[]{:S(2)}) copy-start(bf16[1,128,1024]{2,1,0:T(8,128)(2,1)} %k_hbm.1) | copy-start | bytes 786436
  2.5 0.9 %copy-start.2 = (bf16[1,128,1024]{2,1,0:T(8,128)(2,1)S(1)}, bf16[1,128,1024]{2,1,0:T(8,128)(2,1)}, u32[]{:S(2)}) copy-start(bf16[1,128,1024]{2,1,0:T(8,128)(2,1)} %v_hbm.1) | copy-start | bytes 786436
  3.5 0.8 %copy-start.3 = (bf16[1,32,1024]{2,1,0:T(8,128)(2,1)S(1)}, bf16[1,32,1024]{2,1,0:T(8,128)(2,1)}, u32[]{:S(2)}) copy-start(bf16[1,32,1024]{2,1,0:T(8,128)(2,1)} %cot_hbm.1) | copy-start | bytes 196612
  4.3 0.7 %copy-start.4 = (s32[1,128]{1,0:T(1,128)S(1)}, s32[1,128]{1,0:T(1,128)}, u32[]{:S(2)}) copy-start(s32[1,128]{1,0:T(1,128)} %lev_hbm.1) | copy-start | bytes 1540
  5.0 0.7 %copy-start.5 = (f32[1,128]{1,0:T(1,128)S(1)}, f32[1,128]{1,0:T(1,128)}, u32[]{:S(2)}) copy-start(f32[1,128]{1,0:T(1,128)} %logit_hbm.1) | copy-start | bytes 1540
  5.6 0.7 %copy-start.6 = (f32[8]{0:T(128)S(1)}, f32[8]{0:T(128)}, u32[]{:S(2)}) copy-start(f32[8]{0:T(128)} %mult_ref.1) | copy-start | bytes 100

commit v2 on v1

--- a/solution.py
+++ b/solution.py
@@ -24,7 +24,7 @@
     v_hbm,
     lev_hbm,
     logit_hbm,
-    mult_ref,
+    mult_hbm,
     cot_hbm,
     mixed_ref,
     gg_ref,
@@ -38,6 +38,7 @@
     cot_in,
     lev_in,
     logit_in,
+    mult_in,
     send_a,
     send_b,
     send_c,
@@ -70,7 +71,8 @@
     k_copy = local_copy(k_hbm.at[0], k_in, 3)
     v_copy = local_copy(v_hbm.at[0], v_in, 4)
     cot_copy = local_copy(cot_hbm.at[0], cot_in, 5)
-    for c in (lev_copy, logit_copy, q_copy, k_copy, v_copy, cot_copy):
+    mult_copy = local_copy(mult_hbm, mult_in, 6)
+    for c in (lev_copy, q_copy, k_copy, v_copy, logit_copy, cot_copy, mult_copy):
         c.start()
 
     def peer_loop(f):
@@ -170,7 +172,9 @@
     peer_loop(lambda d: copy_c(d, me).start())
     recv_c[me] = send_c[me]
 
-    temp = mult_ref[me]
+    mult_copy.wait()
+    heads = lax.broadcasted_iota(jnp.int32, mult_in.shape, 1)
+    temp = jnp.sum(jnp.where(heads == me, mult_in[...], 0.0), axis=1, keepdims=True)
     peer_loop(lambda d: copy_a(d, d).wait_recv())
     q_all = recv_a[:, 0:cap, :].reshape(total, hd)
     k_all = recv_a[:, cap : 2 * cap, :].reshape(total, hd)
@@ -312,7 +316,7 @@
     summed = dm_all[0]
     for r in range(1, reps):
         summed = summed + dm_all[r]
-    dm_ref[...] = summed[0:1]
+    dm_ref[...] = summed[0:1, 0:1]
 
     for copy in (copy_v, copy_q, copy_k):
         peer_loop(lambda d: copy(d, d).wait_recv())
@@ -322,12 +326,25 @@
         copy_dm(lax.rem(my_rep + r, reps), my_rep).wait_send()
 
 
+def store(*refs):
+    ins, outs, held, got, put = refs[:6], refs[6:12], refs[12:18], refs[18], refs[19]
+    reads = [pltpu.make_async_copy(ins[i], held[i], got.at[i]) for i in range(6)]
+    writes = [pltpu.make_async_copy(held[i], outs[i], put.at[i]) for i in range(6)]
+    for c in reads:
+        c.start()
+    for r, w in zip(reads, writes):
+        r.wait()
+        w.start()
+    for c in writes:
+        c.wait()
+
+
 def local(n, reps, q, k, v, levels, logits, mult, cot):
     tokens, width = q.shape[1], q.shape[2]
     cap = cot.shape[1]
     hd = width // mult.shape[0]
     total = n * cap
-    anyspec = pl.BlockSpec(memory_space=pl.ANY)
+    far = pl.BlockSpec(memory_space=pltpu.HBM)
     vm = pl.BlockSpec(memory_space=pltpu.VMEM)
     wide = jax.ShapeDtypeStruct((1, cap, width), BF16)
     outs = pl.pallas_call(
@@ -338,9 +355,9 @@
             wide,
             wide,
             wide,
-            jax.ShapeDtypeStruct((1, 128), F32),
+            jax.ShapeDtypeStruct((1, 1), F32),
         ),
-        in_specs=[anyspec] * 5 + [pl.BlockSpec(memory_space=pltpu.SMEM), anyspec],
+        in_specs=[far] * 7,
         out_specs=(vm,) * 6,
         scratch_shapes=[
             pltpu.VMEM((tokens, width), BF16),
@@ -349,6 +366,7 @@
             pltpu.VMEM((cap, width), BF16),
             pltpu.VMEM((1, tokens), jnp.int32),
             pltpu.VMEM((1, tokens), F32),
+            pltpu.VMEM((1, n), F32),
             pltpu.VMEM((n, 2 * cap + 16, hd), BF16),
             pltpu.VMEM((n, cap, hd), BF16),
             pltpu.VMEM((n, cap, hd), BF16),
@@ -361,18 +379,26 @@
             pltpu.VMEM((total, hd), BF16),
             pltpu.VMEM((cap, width), BF16),
             pltpu.VMEM((reps, 8, 128), F32),
-            pltpu.SemaphoreType.DMA((6,)),
+            pltpu.SemaphoreType.DMA((7,)),
             pltpu.SemaphoreType.DMA((7, n)),
             pltpu.SemaphoreType.DMA((7, n)),
             pltpu.SemaphoreType.DMA((reps,)),
             pltpu.SemaphoreType.DMA((reps,)),
         ],
         compiler_params=pltpu.CompilerParams(
-            collective_id=0, has_side_effects=True, vmem_limit_bytes=48 * 1024 * 1024
+            collective_id=0, has_side_effects=True, vmem_limit_bytes=56 * 1024 * 1024
         ),
-    )(q, k, v, levels, logits, mult, cot)
-    mixed, gg, dq, dk, dv, dm = outs
-    return mixed, gg, dq, dk, dv, dm[0, :1]
+    )(q, k, v, levels, logits, mult.reshape(1, n), cot)
+    mixed, gg, dq, dk, dv, dm = pl.pallas_call(
+        store,
+        out_shape=tuple(jax.ShapeDtypeStruct(o.shape, o.dtype) for o in outs),
+        in_specs=[far] * 6,
+        out_specs=(far,) * 6,
+        scratch_shapes=[pltpu.VMEM(o.shape, o.dtype) for o in outs]
+        + [pltpu.SemaphoreType.DMA((6,)), pltpu.SemaphoreType.DMA((6,))],
+        compiler_params=pltpu.CompilerParams(vmem_limit_bytes=56 * 1024 * 1024),
+    )(*outs)
+    return mixed, gg, dq, dk, dv, dm[0]
 
 
 def solution(mesh):

time: 32.5 us -> 25 us (0.77)
  local copies, waits for them, and re-layouts: 8.67 us -> 0 us
  Pallas kernels: 21.7 us -> 24.2 us
  between operations: 1.82 us -> 0.64 us
    unnamed x19 -> x0, local copies, waits for them, and re-layouts: 8.67 us -> none
    pallas_call x0 -> x1, Pallas kernels: none -> 2.36 us  [local(): pl.pallas_call(store, out_shape=tuple((jax.ShapeDtypeStruct(o.shape, o.dt...]
where the time goes in v2:
time: 25 us; the launch traced here: 24.8 us
  Pallas kernels  24.2 us (97%)
  between operations  0.64 us (3%)
    pallas_call x1, Pallas kernels, local(): pl.pallas_call(functools.partial(kernel, n, reps, cap, hd), out_shape=(wi...  21.8 us
    pallas_call x1, Pallas kernels, local(): pl.pallas_call(store, out_shape=tuple((jax.ShapeDtypeStruct(o.shape, o.dt...  2.36 us

profile of v2, /device:TPU:0, one launch (start us, length us, event | category | flops | bytes accessed | tf_op | source)
XLA Modules:
  0.0 24.8 jit_solution(8440500214011885296)
XLA Ops:
  0.6 21.8 %shard_map.118 = (bf16[1,32,1024]{2,1,0:T(8,128)(2,1)}, f32[1,32]{1,0:T(1,128)}, bf16[1,32,1024]{2,1,0:T(8,128)(2,1)}, bf16[1,32,1024]{2,1,0:T(8,128)(2,1)}, bf1...) custom-call(bf16[1,128,1024]{2,1,0:T(8,128)(2,1)} %q_hbm.1, bf16[1,128,1024]{2,1,0:T(8,128)(2,1)} %k_hbm.1, ...), custom_call_target="tpu_custom_call" | custom-call | tf_op jit(solution)/shard_map/pallas_call | solution.py:350
  22.4 2.4 %shard_map.119 = (bf16[1,32,1024]{2,1,0:T(8,128)(2,1)}, f32[1,32]{1,0:T(1,128)}, bf16[1,32,1024]{2,1,0:T(8,128)(2,1)}, bf16[1,32,1024]{2,1,0:T(8,128)(2,1)}, bf1...) custom-call(bf16[1,32,1024]{2,1,0:T(8,128)(2,1)} %get-tuple-element.18.refs_0_, f32[1,32]{1,0:T(1,128)} %get-tuple-element.19.refs_1_, ...), custom_call_target="tpu_custom_call" | custom-call | tf_op jit(solution)/shard_map/pallas_call | solution.py:392

commit v3 on v2

--- a/solution.py
+++ b/solution.py
@@ -26,6 +26,12 @@
     logit_hbm,
     mult_hbm,
     cot_hbm,
+    mixed_hbm,
+    gg_hbm,
+    dq_hbm,
+    dk_hbm,
+    dv_hbm,
+    dm_hbm,
     mixed_ref,
     gg_ref,
     dq_ref,
@@ -178,7 +184,7 @@
     peer_loop(lambda d: copy_a(d, d).wait_recv())
     q_all = recv_a[:, 0:cap, :].reshape(total, hd)
     k_all = recv_a[:, cap : 2 * cap, :].reshape(total, hd)
-    rows = min(total, 256)
+    rows = min(total, 128)
     blocks = total // rows
     lane = lax.broadcasted_iota(jnp.int32, (1, hd), 1)
     per = hd // cap
@@ -227,14 +233,17 @@
         return copy
 
     copy_o = to_slots(3, out_o, attn_in)
-    copy_v = to_slots(4, out_v, dv_ref.at[0])
-    copy_q = to_slots(5, out_q, dq_ref.at[0])
-    copy_k = to_slots(6, out_k, dk_ref.at[0])
-
-    def finish(copy, src, dst):
+    copy_v = to_slots(4, out_v, dv_hbm.at[0])
+    copy_q = to_slots(5, out_q, dq_hbm.at[0])
+    copy_k = to_slots(6, out_k, dk_hbm.at[0])
+
+    def finish(copy, src, dst, sem):
         peer_loop(lambda d: copy(d, me).start())
-        mine = src[pl.ds(pl.multiple_of(me * cap, cap), cap), :]
-        dst[:, pl.ds(pl.multiple_of(me * hd, hd), hd)] = mine
+        return pltpu.make_async_copy(
+            src.at[pl.ds(pl.multiple_of(me * cap, cap), cap), :],
+            dst.at[:, pl.ds(pl.multiple_of(me * hd, hd), hd)],
+            local_sem.at[sem],
+        )
 
     peer_loop(lambda d: copy_b(d, d).wait_recv())
     v_all = recv_b[...].reshape(total, hd)
@@ -243,7 +252,8 @@
         out_o[rb * rows : end, :] = jnp.dot(
             lows[rb], v_all[:end], preferred_element_type=F32
         ).astype(BF16)
-    finish(copy_o, out_o, attn_in)
+    own_o = finish(copy_o, out_o, attn_in, 13)
+    own_o.start()
 
     peer_loop(lambda d: copy_c(d, d).wait_recv())
     u_all = recv_c[...].reshape(total, hd)
@@ -262,7 +272,8 @@
 
     for kb, tile in enumerate(column_sums(lows, u_all)):
         out_v[kb * rows : (kb + 1) * rows, :] = tile.astype(BF16)
-    finish(copy_v, out_v, dv_ref.at[0])
+    own_v = finish(copy_v, out_v, dv_hbm.at[0], 12)
+    own_v.start()
 
     lowered = []
     dm = jnp.zeros((1, 1), F32)
@@ -280,10 +291,12 @@
         out_q[rb * rows : end, :] = jnp.dot(
             low, k_all[:end], preferred_element_type=F32
         ).astype(BF16)
-    finish(copy_q, out_q, dq_ref.at[0])
+    own_q = finish(copy_q, out_q, dq_hbm.at[0], 10)
+    own_q.start()
     for kb, tile in enumerate(column_sums(lowered, q_all)):
         out_k[kb * rows : (kb + 1) * rows, :] = tile.astype(BF16)
-    finish(copy_k, out_k, dk_ref.at[0])
+    own_k = finish(copy_k, out_k, dk_hbm.at[0], 11)
+    own_k.start()
 
     dm_all[my_rep] = jnp.broadcast_to(dm, (8, 128))
 
@@ -300,6 +313,17 @@
     for r in range(1, reps):
         copy_dm(lax.rem(my_rep + r, reps), my_rep).start()
 
+    stores = [
+        local_copy(a, b, 7 + i)
+        for i, (a, b) in enumerate(
+            (
+                (mixed_ref, mixed_hbm),
+                (gg_ref, gg_hbm),
+                (dm_ref, dm_hbm),
+            )
+        )
+    ]
+    own_o.wait()
     peer_loop(lambda d: copy_o(d, d).wait_recv())
     attn = attn_in[...].astype(F32)
     mixed_ref[0] = (gate * attn).astype(BF16)
@@ -309,7 +333,11 @@
         jnp.int32, (cap, cap), 1
     )
     gg_ref[...] = jnp.sum(jnp.where(diagonal, grad_gate, 0.0), axis=0, keepdims=True)
-
+    stores[0].start()
+    stores[1].start()
+
+    for copy in (copy_v, copy_q):
+        peer_loop(lambda d: copy(d, d).wait_recv())
     for r in range(1, reps):
         other = lax.rem(my_rep + r, reps)
         copy_dm(other, other).wait_recv()
@@ -318,12 +346,14 @@
         summed = summed + dm_all[r]
     dm_ref[...] = summed[0:1, 0:1]
 
-    for copy in (copy_v, copy_q, copy_k):
-        peer_loop(lambda d: copy(d, d).wait_recv())
+    stores[2].start()
+    peer_loop(lambda d: copy_k(d, d).wait_recv())
     for copy in (copy_a, copy_b, copy_c, copy_o, copy_v, copy_q, copy_k):
         peer_loop(lambda d: copy(d, me).wait_send())
     for r in range(1, reps):
         copy_dm(lax.rem(my_rep + r, reps), my_rep).wait_send()
+    for c in stores + [own_v, own_q, own_k]:
+        c.wait()
 
 
 def store(*refs):
@@ -345,7 +375,6 @@
     hd = width // mult.shape[0]
     total = n * cap
     far = pl.BlockSpec(memory_space=pltpu.HBM)
-    vm = pl.BlockSpec(memory_space=pltpu.VMEM)
     wide = jax.ShapeDtypeStruct((1, cap, width), BF16)
     outs = pl.pallas_call(
         functools.partial(kernel, n, reps, cap, hd),
@@ -358,8 +387,14 @@
             jax.ShapeDtypeStruct((1, 1), F32),
         ),
         in_specs=[far] * 7,
-        out_specs=(vm,) * 6,
+        out_specs=(far,) * 6,
         scratch_shapes=[
+            pltpu.VMEM((1, cap, width), BF16),
+            pltpu.VMEM((1, cap), F32),
+            pltpu.VMEM((1, cap, width), BF16),
+            pltpu.VMEM((1, cap, width), BF16),
+            pltpu.VMEM((1, cap, width), BF16),
+            pltpu.VMEM((1, 1), F32),
             pltpu.VMEM((tokens, width), BF16),
             pltpu.VMEM((tokens, width), BF16),
             pltpu.VMEM((tokens, width), BF16),
@@ -379,7 +414,7 @@
             pltpu.VMEM((total, hd), BF16),
             pltpu.VMEM((cap, width), BF16),
             pltpu.VMEM((reps, 8, 128), F32),
-            pltpu.SemaphoreType.DMA((7,)),
+            pltpu.SemaphoreType.DMA((14,)),
             pltpu.SemaphoreType.DMA((7, n)),
             pltpu.SemaphoreType.DMA((7, n)),
             pltpu.SemaphoreType.DMA((reps,)),

time: 25 us -> 24.4 us (0.976)
  Pallas kernels: 24.2 us -> 23.6 us
    pallas_call x1, Pallas kernels: 21.8 us -> 21.3 us  [local(): pl.pallas_call(functools.partial(kernel, n, reps, cap, hd), out_shape=(wi...]
where the time goes in v3:
time: 24.4 us; the launch traced here: 24.3 us
  Pallas kernels  23.6 us (97%)
  between operations  0.64 us (3%)
    pallas_call x1, Pallas kernels, local(): pl.pallas_call(functools.partial(kernel, n, reps, cap, hd), out_shape=(wi...  21.3 us
    pallas_call x1, Pallas kernels, local(): pl.pallas_call(store, out_shape=tuple((jax.ShapeDtypeStruct(o.shape, o.dt...  2.36 us

profile of v3, /device:TPU:0, one launch (start us, length us, event | category | flops | bytes accessed | tf_op | source)
XLA Modules:
  0.0 24.3 jit_solution(7033616235221779683)
XLA Ops:
  0.6 21.3 %shard_map.118 = (bf16[1,32,1024]{2,1,0:T(8,128)(2,1)}, f32[1,32]{1,0:T(1,128)}, bf16[1,32,1024]{2,1,0:T(8,128)(2,1)}, bf16[1,32,1024]{2,1,0:T(8,128)(2,1)}, bf1...) custom-call(bf16[1,128,1024]{2,1,0:T(8,128)(2,1)} %q_hbm.1, bf16[1,128,1024]{2,1,0:T(8,128)(2,1)} %k_hbm.1, ...), custom_call_target="tpu_custom_call" | custom-call | tf_op jit(solution)/shard_map/pallas_call | solution.py:379
  21.9 2.4 %shard_map.119 = (bf16[1,32,1024]{2,1,0:T(8,128)(2,1)}, f32[1,32]{1,0:T(1,128)}, bf16[1,32,1024]{2,1,0:T(8,128)(2,1)}, bf16[1,32,1024]{2,1,0:T(8,128)(2,1)}, bf1...) custom-call(bf16[1,32,1024]{2,1,0:T(8,128)(2,1)} %get-tuple-element.18.refs_0_, f32[1,32]{1,0:T(1,128)} %get-tuple-element.19.refs_1_, ...), custom_call_target="tpu_custom_call" | custom-call | tf_op jit(solution)/shard_map/pallas_call | solution.py:427

commit v4 on v3

--- a/solution.py
+++ b/solution.py
@@ -324,6 +324,8 @@
         )
     ]
     own_o.wait()
+    for copy in (copy_a, copy_b, copy_c):
+        peer_loop(lambda d: copy(d, me).wait_send())
     peer_loop(lambda d: copy_o(d, d).wait_recv())
     attn = attn_in[...].astype(F32)
     mixed_ref[0] = (gate * attn).astype(BF16)
@@ -336,6 +338,7 @@
     stores[0].start()
     stores[1].start()
 
+    peer_loop(lambda d: copy_o(d, me).wait_send())
     for copy in (copy_v, copy_q):
         peer_loop(lambda d: copy(d, d).wait_recv())
     for r in range(1, reps):
@@ -347,13 +350,14 @@
     dm_ref[...] = summed[0:1, 0:1]
 
     stores[2].start()
-    peer_loop(lambda d: copy_k(d, d).wait_recv())
-    for copy in (copy_a, copy_b, copy_c, copy_o, copy_v, copy_q, copy_k):
+    for copy in (copy_v, copy_q):
         peer_loop(lambda d: copy(d, me).wait_send())
     for r in range(1, reps):
         copy_dm(lax.rem(my_rep + r, reps), my_rep).wait_send()
     for c in stores + [own_v, own_q, own_k]:
         c.wait()
+    peer_loop(lambda d: copy_k(d, d).wait_recv())
+    peer_loop(lambda d: copy_k(d, me).wait_send())
 
 
 def store(*refs):

time: 24.4 us -> 24.4 us (level)
  no operation moved by 1% of the time
where the time goes in v4:
time: 24.4 us; the launch traced here: 24.2 us
  Pallas kernels  23.5 us (96%)
  between operations  0.64 us (3%)
    pallas_call x1, Pallas kernels, local(): pl.pallas_call(functools.partial(kernel, n, reps, cap, hd), out_shape=(wi...  21.2 us
    pallas_call x1, Pallas kernels, local(): pl.pallas_call(store, out_shape=tuple((jax.ShapeDtypeStruct(o.shape, o.dt...  2.36 us

profile of v4, /device:TPU:0, one launch (start us, length us, event | category | flops | bytes accessed | tf_op | source)
XLA Modules:
  0.0 24.2 jit_solution(1933065097038255086)
XLA Ops:
  0.6 21.2 %shard_map.118 = (bf16[1,32,1024]{2,1,0:T(8,128)(2,1)}, f32[1,32]{1,0:T(1,128)}, bf16[1,32,1024]{2,1,0:T(8,128)(2,1)}, bf16[1,32,1024]{2,1,0:T(8,128)(2,1)}, bf1...) custom-call(bf16[1,128,1024]{2,1,0:T(8,128)(2,1)} %q_hbm.1, bf16[1,128,1024]{2,1,0:T(8,128)(2,1)} %k_hbm.1, ...), custom_call_target="tpu_custom_call" | custom-call | tf_op jit(solution)/shard_map/pallas_call | solution.py:383
  21.8 2.4 %shard_map.119 = (bf16[1,32,1024]{2,1,0:T(8,128)(2,1)}, f32[1,32]{1,0:T(1,128)}, bf16[1,32,1024]{2,1,0:T(8,128)(2,1)}, bf16[1,32,1024]{2,1,0:T(8,128)(2,1)}, bf1...) custom-call(bf16[1,32,1024]{2,1,0:T(8,128)(2,1)} %get-tuple-element.18.refs_0_, f32[1,32]{1,0:T(1,128)} %get-tuple-element.19.refs_1_, ...), custom_call_target="tpu_custom_call" | custom-call | tf_op jit(solution)/shard_map/pallas_call | solution.py:431

commit v5 on v3

--- a/solution.py
+++ b/solution.py
@@ -138,11 +138,11 @@
             dst[c, row : row + cap, :] = part[:, :hd]
             dst[c + 1, row : row + cap, :] = part[:, hd:]
 
-    def to_head(part, src, dst):
+    def to_head(part, src, dst, low, high):
         def copy(d, slot):
             return pltpu.make_async_remote_copy(
-                src_ref=src.at[d],
-                dst_ref=dst.at[slot],
+                src_ref=src.at[d, low:high, :],
+                dst_ref=dst.at[slot, low:high, :],
                 send_sem=send_sem.at[part, d],
                 recv_sem=recv_sem.at[part, slot],
                 device_id={"seq": d},
@@ -151,15 +151,17 @@
 
         return copy
 
-    copy_a = to_head(0, send_a, recv_a)
-    copy_b = to_head(1, send_b, recv_b)
-    copy_c = to_head(2, send_c, recv_c)
+    copy_a = to_head(0, send_a, recv_a, cap, 2 * cap + 16)
+    copy_b = to_head(1, send_b, recv_b, 0, cap)
+    copy_c = to_head(2, send_c, recv_c, 0, cap)
+    copy_d = to_head(7, send_a, recv_a, 0, cap)
 
     q_copy.wait()
     gather(q_in, send_a, 0)
+    pl.semaphore_wait(barrier, n - 1 + reps - 1)
+    peer_loop(lambda d: copy_d(d, me).start())
     k_copy.wait()
     gather(k_in, send_a, cap)
-    pl.semaphore_wait(barrier, n - 1 + reps - 1)
     peer_loop(lambda d: copy_a(d, me).start())
     recv_a[me] = send_a[me]
 
@@ -181,6 +183,7 @@
     mult_copy.wait()
     heads = lax.broadcasted_iota(jnp.int32, mult_in.shape, 1)
     temp = jnp.sum(jnp.where(heads == me, mult_in[...], 0.0), axis=1, keepdims=True)
+    peer_loop(lambda d: copy_d(d, d).wait_recv())
     peer_loop(lambda d: copy_a(d, d).wait_recv())
     q_all = recv_a[:, 0:cap, :].reshape(total, hd)
     k_all = recv_a[:, cap : 2 * cap, :].reshape(total, hd)
@@ -348,7 +351,7 @@
 
     stores[2].start()
     peer_loop(lambda d: copy_k(d, d).wait_recv())
-    for copy in (copy_a, copy_b, copy_c, copy_o, copy_v, copy_q, copy_k):
+    for copy in (copy_d, copy_a, copy_b, copy_c, copy_o, copy_v, copy_q, copy_k):
         peer_loop(lambda d: copy(d, me).wait_send())
     for r in range(1, reps):
         copy_dm(lax.rem(my_rep + r, reps), my_rep).wait_send()
@@ -415,8 +418,8 @@
             pltpu.VMEM((cap, width), BF16),
             pltpu.VMEM((reps, 8, 128), F32),
             pltpu.SemaphoreType.DMA((14,)),
-            pltpu.SemaphoreType.DMA((7, n)),
-            pltpu.SemaphoreType.DMA((7, n)),
+            pltpu.SemaphoreType.DMA((8, n)),
+            pltpu.SemaphoreType.DMA((8, n)),
             pltpu.SemaphoreType.DMA((reps,)),
             pltpu.SemaphoreType.DMA((reps,)),
         ],

time: 24.4 us -> 24.6 us (level)
  no operation moved by 1% of the time
where the time goes in v5:
time: 24.6 us; the launch traced here: 24.4 us
  Pallas kernels  23.8 us (97%)
  between operations  0.64 us (3%)
    pallas_call x1, Pallas kernels, local(): pl.pallas_call(functools.partial(kernel, n, reps, cap, hd), out_shape=(wi...  21.4 us
    pallas_call x1, Pallas kernels, local(): pl.pallas_call(store, out_shape=tuple((jax.ShapeDtypeStruct(o.shape, o.dt...  2.36 us

profile of v5, /device:TPU:0, one launch (start us, length us, event | category | flops | bytes accessed | tf_op | source)
XLA Modules:
  0.0 24.4 jit_solution(9060457657568997736)
XLA Ops:
  0.6 21.4 %shard_map.118 = (bf16[1,32,1024]{2,1,0:T(8,128)(2,1)}, f32[1,32]{1,0:T(1,128)}, bf16[1,32,1024]{2,1,0:T(8,128)(2,1)}, bf16[1,32,1024]{2,1,0:T(8,128)(2,1)}, bf1...) custom-call(bf16[1,128,1024]{2,1,0:T(8,128)(2,1)} %q_hbm.1, bf16[1,128,1024]{2,1,0:T(8,128)(2,1)} %k_hbm.1, ...), custom_call_target="tpu_custom_call" | custom-call | tf_op jit(solution)/shard_map/pallas_call | solution.py:382
  22.0 2.4 %shard_map.119 = (bf16[1,32,1024]{2,1,0:T(8,128)(2,1)}, f32[1,32]{1,0:T(1,128)}, bf16[1,32,1024]{2,1,0:T(8,128)(2,1)}, bf16[1,32,1024]{2,1,0:T(8,128)(2,1)}, bf1...) custom-call(bf16[1,32,1024]{2,1,0:T(8,128)(2,1)} %get-tuple-element.18.refs_0_, f32[1,32]{1,0:T(1,128)} %get-tuple-element.19.refs_1_, ...), custom_call_target="tpu_custom_call" | custom-call | tf_op jit(solution)/shard_map/pallas_call | solution.py:430
